TPU v7x, 1024 devices: a whole 4x8x16 slice. The times are simulated.
1024 devices in a mesh: outer: 4 (over x), dp: 32 (over z, core), tensor: 8 (over y).
Axes of the slice: x: 4, y: 8, z: 16, core: 2. Of those that a mesh axis runs over, the one named last changes fastest.
Arguments:
- tokens: bfloat16 [49152, 1024], P(('outer', 'dp'), 'tensor'), may hold values from -8 to 8
- input_weight: bfloat16 [1024, 3, 1024], P(None, None, 'tensor'), may hold values from -1 to 1
- output_weight: bfloat16 [1024, 1024], P('tensor'), may hold values from -0.1875 to 0.1875
- grad_layer: bfloat16 [49152, 1024], P(('outer', 'dp'), 'tensor'), may hold values from -6 to 6
- patch_blocks: int32 [128, 3], replicated, may hold values from 1 to 2, as said below
- target_group: int32 [128, 3], replicated, may hold values from 0 to 31, as said below
Outputs:
- layer_out: bfloat16 [49152, 1024], P(('outer', 'dp'), 'tensor')
- grad_tokens: bfloat16 [49152, 1024], P(('outer', 'dp'), 'tensor')
- grad_input_weight: float32 [1024, 3, 1024], P(None, None, 'tensor')
- grad_output_weight: float32 [1024, 1024], P('tensor')
Inputs may be any that keep to these rules, and one draw needn't show every extreme that they name: Image i of group g has 64 * patch_blocks[g, i] patches; a group's images lie one after another from its first row. `target_group`: the index along dp of the group that takes image i of group g, within g's index along outer. A group hands at most one image to other groups and takes at most one from them, and after the moves each group's images fit in 384 rows.
All inputs are finite; a program needn't handle non-finite values.
Results may differ from a plain program's by a relative error of at most 0.02.
Values may be sent and summed in bfloat16 or wider, within the bound.
A program may use at most 32 MiB of HBM per device.

v0:
```python
import jax
import jax.numpy as jnp
from jax import lax
from jax.sharding import PartitionSpec as P

D = 1024
HEADS = 16
BLOCK = 64
LEN_MAX = 2


def layout(group_blocks, group_dest, place, row_count, capacity):
    group_count, image_count = group_blocks.shape
    sources = jnp.arange(group_count, dtype=jnp.int32)
    picked = (sources == place)[:, None]
    lens_all = BLOCK * group_blocks
    starts_all = jnp.cumsum(lens_all, axis=1) - lens_all
    own_len = jnp.sum(jnp.where(picked, lens_all, 0), axis=0)
    own_start = jnp.sum(jnp.where(picked, starts_all, 0), axis=0)
    own_dest = jnp.sum(jnp.where(picked, group_dest, 0), axis=0)
    staying = own_dest == place
    kept_len = jnp.where(staying, own_len, 0)
    dst_off = jnp.cumsum(kept_len) - kept_len
    kept_total = jnp.sum(kept_len)
    out_len = jnp.sum(jnp.where(staying, 0, own_len))
    out_start = jnp.sum(jnp.where(staying, 0, own_start))
    target_peer = jnp.sum(jnp.where(staying, 0, own_dest))
    coming = (group_dest == place) & (group_dest != sources[:, None])
    in_len = jnp.sum(jnp.where(coming, lens_all, 0))
    source_peer = jnp.sum(jnp.where(coming, sources[:, None], 0))
    in_start = jnp.sum(jnp.where(coming, starts_all, 0))
    seg_off = jnp.concatenate([dst_off, kept_total[None]])
    seg_len = jnp.concatenate([kept_len, in_len[None]])
    position = jnp.arange(row_count, dtype=jnp.int32)
    inside = (position[:, None] >= seg_off[None, :]) & (
        position[:, None] < (seg_off + seg_len)[None, :]
    )
    segment_marks = jnp.arange(image_count + 1, dtype=jnp.int32)
    segment = jnp.sum(jnp.where(inside, segment_marks[None, :], 0), axis=1)
    live = jnp.any(inside, axis=1)
    offset_in = position - jnp.sum(jnp.where(inside, seg_off[None, :], 0), axis=1)
    own_src = jnp.sum(jnp.where(inside[:, :image_count], own_start[None, :], 0), axis=1)
    pull = jnp.where(segment < image_count, own_src + offset_in, row_count + offset_in)
    pull = jnp.where(live, pull, row_count + capacity)
    own_inside = (position[:, None] >= own_start[None, :]) & (
        position[:, None] < (own_start + own_len)[None, :]
    )
    target = jnp.where(staying, dst_off - own_start, row_count - own_start)
    back = position + jnp.sum(jnp.where(own_inside, target[None, :], 0), axis=1)
    back = jnp.where(jnp.any(own_inside, axis=1), back, row_count + capacity)
    slot_index = jnp.arange(capacity, dtype=jnp.int32)
    send = jnp.where(slot_index < out_len, out_start + slot_index, row_count)
    reply = jnp.where(slot_index < in_len, kept_total + slot_index, row_count)
    block_ok = slot_index[None, :] < seg_len[:, None]
    block_rows = jnp.where(block_ok, seg_off[:, None] + slot_index[None, :], row_count)
    flat_back = jnp.where(live, segment * capacity + offset_in, (image_count + 1) * capacity)
    return {
        "segment": segment,
        "live": live,
        "offset_in": offset_in,
        "own_src": own_src,
        "pull": pull,
        "back": back,
        "send": send,
        "reply": reply,
        "block_ok": block_ok,
        "block_rows": block_rows,
        "flat_back": flat_back,
        "out_len": out_len,
        "in_len": in_len,
        "target_peer": target_peer,
        "source_peer": source_peer,
        "in_start": in_start,
    }


def attend(queries, key_rows, value_rows, allowed, row_ok):
    scores = (
        jnp.einsum("blhd,bmhd->bhlm", queries, key_rows, preferred_element_type=jnp.float32) * 0.125
    )
    allowed_heads = allowed[:, None]
    scores = jnp.where(allowed_heads, scores, -1e30)
    row_peak = jnp.max(scores, axis=-1, keepdims=True)
    weights = jnp.exp(scores - row_peak) * allowed_heads.astype(jnp.float32)
    totals = jnp.sum(weights, axis=-1, keepdims=True)
    totals = jnp.where(row_ok[:, None, :, None], totals, 1.0)
    shares = weights / totals
    shares_low = shares.astype(jnp.bfloat16)
    attended = jnp.einsum(
        "bhlm,bmhd->blhd", shares_low, value_rows, preferred_element_type=jnp.float32
    )
    return (attended.astype(jnp.bfloat16), shares, shares_low)


def attend_back(queries, key_rows, value_rows, shares, shares_low, grad_attended):
    grad_shares = jnp.einsum(
        "blhd,bmhd->bhlm", grad_attended, value_rows, preferred_element_type=jnp.float32
    )
    inner_sum = jnp.sum(shares * grad_shares, axis=-1, keepdims=True)
    grad_scores = (0.125 * shares * (grad_shares - inner_sum)).astype(jnp.bfloat16)
    grad_query = jnp.einsum(
        "bhlm,bmhd->blhd", grad_scores, key_rows, preferred_element_type=jnp.float32
    )
    grad_key = jnp.einsum(
        "bhlm,blhd->bmhd", grad_scores, queries, preferred_element_type=jnp.float32
    )
    grad_value = jnp.einsum(
        "bhlm,blhd->bmhd", shares_low, grad_attended, preferred_element_type=jnp.float32
    )
    return jnp.stack(
        [
            grad_query.astype(jnp.bfloat16),
            grad_key.astype(jnp.bfloat16),
            grad_value.astype(jnp.bfloat16),
        ],
        axis=2,
    )


def on_device(tokens, input_weight, output_weight, grad_layer, patch_blocks, target_group):
    row_count, narrow = tokens.shape
    group_count = lax.axis_size("dp")
    group_place = lax.axis_index("dp")
    outer_place = lax.axis_index("outer")
    image_count = patch_blocks.shape[1]
    capacity = LEN_MAX * BLOCK
    head_dim = D // HEADS
    heads_here = narrow // head_dim
    group_blocks = lax.dynamic_slice_in_dim(patch_blocks, outer_place * group_count, group_count, 0)
    group_dest = lax.dynamic_slice_in_dim(target_group, outer_place * group_count, group_count, 0)
    arrangement = layout(group_blocks, group_dest, group_place, row_count, capacity)
    zero_row = jnp.zeros((1, narrow), jnp.bfloat16)
    peer_index = jnp.arange(group_count, dtype=jnp.int32)
    outgoing = jnp.take(jnp.concatenate([tokens, zero_row]), arrangement["send"], axis=0)
    aimed_slot = (peer_index == arrangement["target_peer"]) & (arrangement["out_len"] > 0)
    parcel = jnp.where(aimed_slot[:, None, None], outgoing[None], jnp.zeros_like(outgoing)[None])
    arrived = lax.all_to_all(parcel, "dp", split_axis=0, concat_axis=0, tiled=True)
    incoming = lax.dynamic_index_in_dim(arrived, arrangement["source_peer"], 0, keepdims=False)
    arranged = jnp.take(jnp.concatenate([tokens, incoming, zero_row]), arrangement["pull"], axis=0)
    full_tokens, full_grad = (
        lax.all_gather(arranged, "tensor", axis=1, tiled=True),
        lax.all_gather(grad_layer, "tensor", axis=1, tiled=True),
    )
    model_width = full_tokens.shape[1]
    projected = jnp.dot(
        full_tokens,
        input_weight.reshape(model_width, 3 * narrow),
        preferred_element_type=jnp.float32,
    )
    projected = projected.astype(jnp.bfloat16).reshape(row_count, 3, heads_here, head_dim)
    grad_attended = jnp.einsum(
        "rd,cd->rc", full_grad, output_weight, preferred_element_type=jnp.float32
    )
    grad_attended = grad_attended.astype(jnp.bfloat16).reshape(row_count, heads_here, head_dim)
    block_count = image_count + 1
    block_index = arrangement["block_rows"].reshape(-1)
    padded_proj = jnp.concatenate(
        [projected, jnp.zeros((1, 3, heads_here, head_dim), jnp.bfloat16)]
    )
    proj_blocks = jnp.take(padded_proj, block_index, axis=0).reshape(
        block_count, capacity, 3, heads_here, head_dim
    )
    padded_grad = jnp.concatenate(
        [grad_attended, jnp.zeros((1, heads_here, head_dim), jnp.bfloat16)]
    )
    grad_blocks = jnp.take(padded_grad, block_index, axis=0).reshape(
        block_count, capacity, heads_here, head_dim
    )
    block_ok = arrangement["block_ok"]
    allowed = block_ok[:, :, None] & block_ok[:, None, :]
    attended, shares, shares_low = attend(
        proj_blocks[:, :, 0], proj_blocks[:, :, 1], proj_blocks[:, :, 2], allowed, block_ok
    )
    gradients = attend_back(
        proj_blocks[:, :, 0],
        proj_blocks[:, :, 1],
        proj_blocks[:, :, 2],
        shares,
        shares_low,
        grad_blocks,
    )
    flat_back = arrangement["flat_back"]
    attended_rows = jnp.take(
        jnp.concatenate([attended.reshape(block_count * capacity, narrow), zero_row]),
        flat_back,
        axis=0,
    )
    grad_rows = jnp.take(
        jnp.concatenate(
            [
                gradients.reshape(block_count * capacity, 3, narrow),
                jnp.zeros((1, 3, narrow), jnp.bfloat16),
            ]
        ),
        flat_back,
        axis=0,
    )
    out_term = jnp.dot(attended_rows, output_weight, preferred_element_type=jnp.float32)
    back_term = jnp.einsum(
        "rjc,djc->rd", grad_rows, input_weight, preferred_element_type=jnp.float32
    )
    out_sum, back_sum = (
        lax.psum_scatter(
            out_term.astype(jnp.bfloat16), "tensor", scatter_dimension=1, tiled=True
        ).astype(jnp.float32),
        lax.psum_scatter(
            back_term.astype(jnp.bfloat16), "tensor", scatter_dimension=1, tiled=True
        ).astype(jnp.float32),
    )
    layer_out = out_sum.astype(jnp.bfloat16)
    grad_target = back_sum.astype(jnp.bfloat16)
    term_input = jnp.einsum(
        "rd,rjc->djc", full_tokens, grad_rows, preferred_element_type=jnp.float32
    )
    term_output = jnp.einsum(
        "rc,rd->cd", attended_rows, full_grad, preferred_element_type=jnp.float32
    )
    grad_input_weight, grad_output_weight = lax.psum((term_input, term_output), ("outer", "dp"))
    answer = jnp.take(jnp.concatenate([grad_target, zero_row]), arrangement["reply"], axis=0)
    aimed_back = (peer_index == arrangement["source_peer"]) & (arrangement["in_len"] > 0)
    parcel_back = jnp.where(aimed_back[:, None, None], answer[None], jnp.zeros_like(answer)[None])
    answers_all = lax.all_to_all(parcel_back, "dp", split_axis=0, concat_axis=0, tiled=True)
    returned = lax.dynamic_index_in_dim(answers_all, arrangement["target_peer"], 0, keepdims=False)
    grad_tokens = jnp.take(
        jnp.concatenate([grad_target, returned, zero_row]), arrangement["back"], axis=0
    )
    return (layer_out, grad_tokens, grad_input_weight, grad_output_weight)


def solution(mesh):
    return jax.shard_map(
        on_device,
        mesh=mesh,
        in_specs=(
            P(("outer", "dp"), "tensor"),
            P(None, None, "tensor"),
            P("tensor", None),
            P(("outer", "dp"), "tensor"),
            P(),
            P(),
        ),
        out_specs=(
            P(("outer", "dp"), "tensor"),
            P(("outer", "dp"), "tensor"),
            P(None, None, "tensor"),
            P("tensor", None),
        ),
        check_vma=False,
    )
```

profile of v0, /device:TPU:1, one launch (start us, length us, event | category | flops | bytes accessed | tf_op | source)
XLA Modules:
  0.0 581.5 jit_solution(14119396890250603509)
XLA Ops:
  8.0 0.8 dynamic-slice_multiply_fusion
  8.9 1.4 select_reduce_fusion.4
  10.3 1.4 select_reduce_fusion.5
  11.7 0.6 fusion.37
  12.5 0.7 select_reduce_fusion.9
  13.9 3.2 compare_and_fusion.1
  17.1 0.7 compare_and_fusion.6
  17.8 0.9 concatenate.41
  18.7 0.7 gather_fusion.3
  19.5 1.1 broadcast_select_fusion.1
  20.6 20.6 %all-to-all-start = ((bf16[32,128,128]{2,1,0:T(8,128)(2,1)}), bf16[32,128,128]{2,1,0:T(8,128)(2,1)S(1)}, u32[]{:S(2)}, u32[]{:S(2)}) async-start(bf16[32,128,128]{2,1,0:T(8,128)(2,1)} %broadcast_select_fusion.1), calls=%async_computation | async-start | bytes 2097152 | tf_op jit(solution)/shard_map/all_to_all | solution.py:137
  42.5 1.2 copy.62
  43.7 24.1 %all_gather.7 = bf16[384,1024]{1,0:T(8,128)(2,1)S(1)} all-gather(bf16[384,128]{1,0:T(8,128)(2,1)S(1)} %copy-done.13), channel_id=1, replica_groups=mesh['outer'=4,'dp'=32,'tensor'=8] {'tensor'}, dimensions={1}, use_global_device_ids=true | all-gather | bytes 884736 | tf_op jit(solution)/shard_map/all_gather | solution.py:142
  68.6 1.4 fusion.36
  70.1 2.1 gather_fusion.1
  73.4 0.7 broadcast_select_fusion.4
  74.1 0.8 broadcast_and_fusion
  75.0 21.9 %all-to-all-done = bf16[32,128,128]{2,1,0:T(8,128)(2,1)S(1)} async-done(((bf16[32,128,128]{2,1,0:T(8,128)(2,1)}), bf16[32,128,128]{2,1,0:T(8,128)(2,1)S(1)}, u32[]{:S(2)}, u32[]{:S(2)}) %all-to-all-start) | async-done | bytes 1048608 | tf_op jit(solution)/shard_map/all_to_all | solution.py:137
  97.0 1.4 gather_fusion.4
  98.7 22.6 %all_gather.6 = bf16[384,1024]{0,1:T(8,128)(2,1)S(1)} all-gather(bf16[384,128]{0,1:T(8,128)(2,1)S(1)} %broadcast_select_fusion.7), channel_id=1, replica_groups=mesh['outer'=4,'dp'=32,'tensor'=8] {'tensor'}, dimensions={1}, use_global_device_ids=true | all-gather | bytes 884736 | tf_op jit(solution)/shard_map/all_gather | solution.py:141
  121.3 0.9 copy-done.2
  122.2 0.6 convolution_convert_fusion.1
  123.3 0.6 concatenate.43
  124.0 3.2 gather_fusion
  127.2 1.0 copy.65
  131.6 0.9 fusion.15
  132.5 2.0 gather_fusion.2
  134.6 1.3 broadcast_select_fusion.2
  135.9 0.6 bitcast_convert_fusion
  136.5 1.2 copy.97
  138.3 0.7 compare_and_fusion.5
  139.0 34.4 %reduce-scatter.9.cloned.1.call-done = bf16[128,384]{1,0:T(8,128)(2,1)} async-done(((bf16[1024,384]{1,0:T(8,128)(2,1)}), bf16[128,384]{1,0:T(8,128)(2,1)}) %reduce-scatter.9.cloned.1.call-update) | async-done | bytes 98320
  173.4 1.0 copy.98
  174.4 0.7 gather_fusion.6
  175.2 1.1 broadcast_select_fusion
  176.3 18.9 %all-to-all-start.1 = ((bf16[32,128,128]{2,1,0:T(8,128)(2,1)}), bf16[32,128,128]{2,1,0:T(8,128)(2,1)S(1)}, u32[]{:S(2)}, u32[]{:S(2)}) async-start(bf16[32,128,128]{2,1,0:T(8,128)(2,1)} %broadcast_select_fusion), calls=%async_computation.1 | async-start | bytes 2097152 | tf_op jit(solution)/shard_map/all_to_all | solution.py:222
  196.2 1.4 gather_fusion.5
  198.1 1.2 copy.95
  199.3 1.2 fusion.23
  200.5 1.8 fusion.12
  204.5 34.4 %reduce-scatter.7.cloned.1.call-done = bf16[128,384]{1,0:T(8,128)(2,1)} async-done(((bf16[1024,384]{1,0:T(8,128)(2,1)}), bf16[128,384]{1,0:T(8,128)(2,1)}) %reduce-scatter.7.cloned.1.call-update) | async-done | bytes 98320
  238.9 1.6 copy.96
  240.5 11.8 %all-to-all-done.1 = bf16[32,128,128]{2,1,0:T(8,128)(2,1)S(1)} async-done(((bf16[32,128,128]{2,1,0:T(8,128)(2,1)}), bf16[32,128,128]{2,1,0:T(8,128)(2,1)S(1)}, u32[]{:S(2)}, u32[]{:S(2)}) %all-to-all-start.1) | async-done | bytes 1048608 | tf_op jit(solution)/shard_map/all_to_all | solution.py:222
  252.5 1.4 gather_fusion.7
  253.9 0.8 broadcast_select_fusion.5
  254.7 315.9 %all-reduce.9.cloned.1.call-done = (f32[1024,3,128]{2,0,1:T(8,128)}, f32[128,1024]{1,0:T(8,128)}) async-done(((f32[1024,3,128]{2,0,1:T(8,128)}, f32[128,1024]{1,0:T(8,128)}), (f32[1024,3,128]{2,0,1:T(8,128)}, f32[128,1024]{1,0:T(8,128)})) %all-reduce.9.cloned.1.call-update) | async-done | bytes 2097168 | tf_op jit(solution)/shard_map/psum | solution.py:218
  570.6 2.7 copy.115
  573.3 0.8 copy.116
  (90 shorter events, 7.6 us)
Async XLA Ops:
  8.0 59.8 %copy-start = (bf16[128,1024]{1,0:T(8,128)(2,1)S(1)}, bf16[128,1024]{1,0:T(8,128)(2,1)}, u32[]{:S(2)}) copy-start(bf16[128,1024]{1,0:T(8,128)(2,1)} %param.12) | copy-start | bytes 786436
  20.6 21.9 %copy-start.1 = (bf16[1024,3,128]{2,0,1:T(8,128)(2,1)S(1)}, bf16[1024,3,128]{2,0,1:T(8,128)(2,1)}, u32[]{:S(2)}) copy-start(bf16[1024,3,128]{2,0,1:T(8,128)(2,1)} %param.11) | copy-start | bytes 2359300
  20.6 76.3 %all-to-all-start = ((bf16[32,128,128]{2,1,0:T(8,128)(2,1)}), bf16[32,128,128]{2,1,0:T(8,128)(2,1)S(1)}, u32[]{:S(2)}, u32[]{:S(2)}) async-start(bf16[32,128,128]{2,1,0:T(8,128)(2,1)} %broadcast_select_fusion.1), calls=%async_computation | async-start | bytes 2097152 | tf_op jit(solution)/shard_map/all_to_all | solution.py:137
  41.2 2.6 copy-start.13
  41.2 132.2 %reduce-scatter.9.cloned.1.call-start = ((), (), s32[]{:S(2)}) async-start(), calls=%async_computation.5 | async-start | bytes 884736
  68.4 28.5 %copy-start.10 = (bf16[384,128]{1,0:T(8,128)(2,1)S(1)}, bf16[384,128]{1,0:T(8,128)(2,1)}, u32[]{:S(2)}) copy-start(bf16[384,128]{1,0:T(8,128)(2,1)} %param.10) | copy-start | bytes 294916
  97.0 25.1 %copy-start.8 = (bf16[1024,3,128]{0,2,1:T(8,128)(2,1)S(1)}, bf16[1024,3,128]{0,2,1:T(8,128)(2,1)}, u32[]{:S(2)}) copy-start(bf16[1024,3,128]{0,2,1:T(8,128)(2,1)} %copy.62) | copy-start | bytes 2359300
  121.3 0.9 copy-start.2
  127.2 1.1 copy-start.11
  128.2 0.9 copy-start.12
  128.3 2.1 copy-start.6
  135.9 1.8 copy-start.4
  136.5 2.5 copy-start.14
  176.3 18.9 %copy-start.7 = (bf16[4,128,3,2,64]{1,4,3,0,2:T(8,128)(2,1)S(1)}, bf16[4,128,3,2,64]{1,4,3,0,2:T(8,128)(2,1)}, u32[]{:S(2)}) copy-start(bf16[4,128,3,2,64]{1,4,3,0,2:T(8,128)(2,1)} %copy-done.6) | copy-start | bytes 1179652
  176.3 76.0 %all-to-all-start.1 = ((bf16[32,128,128]{2,1,0:T(8,128)(2,1)}), bf16[32,128,128]{2,1,0:T(8,128)(2,1)S(1)}, u32[]{:S(2)}, u32[]{:S(2)}) async-start(bf16[32,128,128]{2,1,0:T(8,128)(2,1)} %broadcast_select_fusion), calls=%async_computation.1 | async-start | bytes 2097152 | tf_op jit(solution)/shard_map/all_to_all | solution.py:222
  195.2 43.7 %reduce-scatter.7.cloned.1.call-start = ((), (), s32[]{:S(2)}) async-start(), calls=%async_computation.4 | async-start | bytes 884736
  199.2 1.3 copy-start.3
  199.2 1.3 copy-start.5
  199.3 371.3 %all-reduce.9.cloned.1.call-start = ((), (), s32[]{:S(2)}) async-start(), calls=%async_computation.6 | async-start | bytes 4194304 | tf_op jit(solution)/shard_map/psum | solution.py:218
  570.6 2.7 copy-start.9
Sparse Core Ops, SparseCore 0:
  137.8 35.5 reduce-scatter.8
  199.9 38.9 reduce-scatter.6
Sparse Core Ops, SparseCore 1:
  203.8 366.8 all-reduce.8
where the time goes:
time: 582 us
  waiting for transfers between devices  418 us (72%)
  blocking collectives  46.7 us (8%)
  starting transfers between devices  39.6 us (7%)
  local copies, waits for them, and re-layouts  29.3 us (5%)
  between operations  21.4 us (4%)
  other arithmetic  19 us (3%)
  matrix products  7.2 us (1%)
    psum x1, waiting for transfers between devices, on_device(): lax.psum((term_input, term_output), ('outer', 'dp'))  316 us
    unnamed x5, waiting for transfers between devices  68.8 us
    all_gather x1, blocking collectives, on_device(): lax.all_gather(grad_layer, 'tensor', axis=1, tiled=True)  24.1 us
    all_gather x1, blocking collectives, on_device(): lax.all_gather(arranged, 'tensor', axis=1, tiled=True)  22.6 us
    all_to_all x1, waiting for transfers between devices, on_device(): lax.all_to_all(parcel, 'dp', split_axis=0, concat_axis=0, tiled=True)  21.9 us
    all_to_all x1, starting transfers between devices, on_device(): lax.all_to_all(parcel, 'dp', split_axis=0, concat_axis=0, tiled=True)  20.6 us
    all_to_all x1, starting transfers between devices, on_device(): lax.all_to_all(parcel_back, 'dp', split_axis=0, concat_axis=0, tiled=True)  18.9 us
    all_to_all x1, waiting for transfers between devices, on_device(): lax.all_to_all(parcel_back, 'dp', split_axis=0, concat_axis=0, tiled=True)  11.8 us
  transfers between devices with their start and end apart: 5, of which 5 were waited for; matrix products, arithmetic and copies ran while one was open for 3% of the time, Pallas kernels for 0%

commit v1 on v0

v1 whole, which is shorter than its diff:
```python
import jax
import jax.numpy as jnp
from jax import lax
from jax.experimental import pallas as pl
from jax.experimental.pallas import tpu as pltpu
from jax.sharding import PartitionSpec as P

MESH = pl.DeviceIdType.MESH
BF16 = jnp.bfloat16
F32 = jnp.float32

ROWS = 384
NARROW = 128
BLOCK = 64
BLOCKS = 6
IMG = 3
CAP = 128
NT = 8
NZ = 16
NX = 4
NDP = 32
HALF = ROWS // 2
EXTRA = ROWS + CAP
WINDOWS = (0, 64, 128)


def dot(a, b, ca=1, cb=0):
    return lax.dot_general(a, b, (((ca,), (cb,)), ((), ())), preferred_element_type=F32)


def one_if(condition):
    return jnp.where(condition, 1.0, 0.0)


def count(shape, axis):
    return lax.broadcasted_iota(jnp.int32, shape, axis).astype(F32)


def copy_to(src, dst, send, recv, **device):
    return pltpu.make_async_remote_copy(
        src_ref=src,
        dst_ref=dst,
        send_sem=send,
        recv_sem=recv,
        device_id=device,
        device_id_type=MESH,
    )


def kernel(
    tok, wi, wo, gl, pb, tg,
    lay_o, gtok_o, giw_o, gow_o,
    tf, gf, pg, pa, move, qkv, ga, shares, att, attx, gcat, gacc,
    part, csum, crecv, xrecv, tsum, zrecv, full,
    pback, pout, rback, rout,
    ring_s, ring_r, img_s, img_r, zg_s, zg_r, za_s, za_r, sib_s, sib_r,
    core_s, core_r, xr_s, xr_r, zr_s, zr_r, zb_s, zb_r, xb_s, xb_r, cb_s, cb_r,
    rs_s, rs_r,
):
    o = lax.axis_index("outer")
    d = lax.axis_index("dp")
    t = lax.axis_index("tensor")
    z = lax.div(d, 2)
    c = lax.rem(d, 2)
    sibling = d + 1 - 2 * c

    def yat(k):
        return lax.rem(t + (k + NT), NT)

    def zat(k):
        return lax.rem(z + (k + NZ), NZ)

    def xat(k):
        return lax.rem(o + k, NX)

    pending = []

    def go(cp):
        cp.start()
        pending.append(cp)

    barrier = pltpu.get_barrier_semaphore()

    def greet(**device):
        pl.semaphore_signal(barrier, inc=1, device_id=device, device_id_type=MESH)

    for k in range(1, NZ):
        greet(dp=2 * zat(k) + c)
    greet(dp=sibling)
    for k in range(1, NT):
        greet(tensor=yat(k))
    for k in range(1, NX):
        greet(outer=xat(k))

    here = d.astype(F32)
    group = (o * NDP + d).astype(F32)
    lane3 = count((IMG, NARROW), 1)
    blocks_all = pb[...].astype(F32)
    dest_all = tg[...].astype(F32)
    own = one_if(lane3 == group)
    length3 = jnp.sum(blocks_all * own, axis=1, keepdims=True)
    dest3 = jnp.sum(dest_all * own, axis=1, keepdims=True)
    length = [length3[i : i + 1] for i in range(IMG)]
    dest = [dest3[i : i + 1] for i in range(IMG)]
    first = [jnp.zeros((1, 1), F32), length[0], length[0] + length[1]]
    total = first[2] + length[2]
    stays = [one_if(dest[i] == here) for i in range(IMG)]
    moved = [1.0 - stays[i] for i in range(IMG)]
    kept = [stays[i] * length[i] for i in range(IMG)]
    place = [jnp.zeros((1, 1), F32), kept[0], kept[0] + kept[1]]
    kept_total = place[2] + kept[2]
    target = moved[0] * dest[0] + moved[1] * dest[1] + moved[2] * dest[2]

    cut = one_if(count((CAP, ROWS), 1) == count((CAP, ROWS), 0) + BLOCK * kept_total)
    pg[c, z] = dot(cut.astype(BF16), gl[...]).astype(BF16)
    tf[t] = tok[...]
    gf[t, :ROWS, :] = gl[...]

    pl.semaphore_wait(barrier, (NZ - 1) + 1 + (NT - 1) + (NX - 1))

    def gather_z(buf, ss, rs, n):
        def msg(a, j, half=None):
            k = (a + j) % NZ
            sem = NZ if half == 1 else k
            ref = buf.at[c, zat(-a)]
            if half is not None:
                ref = ref.at[pl.ds(half * BLOCK, BLOCK)]
            return copy_to(ref, ref, ss.at[sem], rs.at[sem], dp=2 * zat(j) + c)

        def arrived(k, half=None):
            sem = NZ if half == 1 else k
            ref = buf.at[c, zat(-k)]
            if half is not None:
                ref = ref.at[pl.ds(half * BLOCK, BLOCK)]
            copy_to(ref, ref, ss.at[sem], rs.at[sem], dp=2 * zat(k) + c).wait_recv()

        def one():
            for j in (6, -6, 3, -3, 1, -1):
                go(msg(0, j))

        def two():
            arrived(3)
            go(msg(3, 1))
            go(msg(3, -1))
            arrived(13)
            go(msg(-3, -1))
            go(msg(-3, 1))

        def three():
            arrived(6)
            go(msg(6, 2, 0))
            go(msg(6, 1))
            go(msg(6, -1))
            arrived(10)
            go(msg(-6, -2, 1))
            go(msg(-6, -1))
            go(msg(-6, 1))

        def cross():
            return copy_to(buf.at[c], buf.at[c], sib_s.at[n], sib_r.at[n], dp=sibling)

        def four():
            for k in (1, 15, 2, 14, 4, 12, 5, 11, 7, 9):
                arrived(k)
            arrived(8, 0)
            arrived(8, 1)
            go(cross())

        def five():
            cross().wait_recv()

        return one, two, three, four, five

    zg = gather_z(pg, zg_s, zg_r, 0)
    za = gather_z(pa, za_s, za_r, 1)

    def ring_msg(step, way, buf, n, half):
        slot = yat(-way * (step - 1))
        ref = buf.at[slot, pl.ds(half * HALF, HALF)]
        sem = ((step - 1) * 2 + (way + 1) // 2) * 4 + n * 2 + half
        return copy_to(ref, ref, ring_s.at[sem], ring_r.at[sem], tensor=yat(way))

    def ring_sends(step):
        for half in range(2):
            for n, buf in enumerate((tf, gf)):
                for way in (1, -1):
                    if step < 4 or half == (1 - way) // 2:
                        go(ring_msg(step, way, buf, n, half))

    def ring_waits(step):
        for half in range(2):
            for n, buf in enumerate((tf, gf)):
                for way in (1, -1):
                    if step < 4 or half == (1 - way) // 2:
                        slot = yat(-way * step)
                        ref = buf.at[slot, pl.ds(half * HALF, HALF)]
                        sem = ((step - 1) * 2 + (way + 1) // 2) * 4 + n * 2 + half
                        copy_to(
                            ref, ref, ring_s.at[sem], ring_r.at[sem], tensor=yat(way)
                        ).wait_recv()
                        if step < 3 or (step == 3 and half == (1 - way) // 2):
                            go(ring_msg(step + 1, way, buf, n, half))

    zg[0]()
    ring_sends(1)
    zg[1]()
    ring_waits(1)
    zg[2]()
    ring_waits(2)
    zg[3]()
    zg[4]()

    def pick(buf, peer):
        acc = jnp.zeros((CAP, NARROW), BF16)
        for k in range(NDP):
            mark = jnp.broadcast_to(one_if(peer == float(k)), (1, NARROW)).astype(BF16)
            acc = acc + buf[k % 2, k // 2] * mark
        return acc

    gf[t, ROWS:, :] = pick(pg, target)
    img_ref = gf.at[t, pl.ds(ROWS, CAP)]
    for k in (4, 3, 5, 2, 6, 1, 7):
        go(copy_to(img_ref, img_ref, img_s.at[k], img_r.at[k], tensor=yat(k)))
    ring_waits(3)
    ring_waits(4)

    tokens = jnp.concatenate([tf[n] for n in range(NT)], axis=1)
    for j in range(3):
        qkv[j] = dot(tokens, wi[j]).astype(BF16)

    lane = lax.broadcasted_iota(jnp.int32, (1, NARROW), 1)
    low = lane < BLOCK
    zero = jnp.zeros((), F32)

    def two_heads(x):
        x = x.astype(F32)
        return jnp.concatenate(
            [jnp.where(low, x, zero).astype(BF16), jnp.where(low, zero, x).astype(BF16)], axis=0
        )

    def one_head(x):
        return jnp.where(low, x[:CAP], x[CAP:])

    row = count((ROWS, 1), 0)
    column = jnp.full((ROWS, 1), -1.0, F32)
    for i in range(IMG):
        inside = one_if(row >= BLOCK * first[i]) * one_if(row < BLOCK * (first[i] + length[i]))
        shift = BLOCK * (stays[i] * place[i] + moved[i] * BLOCKS - first[i])
        column = column + inside * (row + shift + 1.0)
    move[...] = one_if(count((ROWS, EXTRA), 1) == column).astype(BF16)

    def image_of(position):
        marks = jnp.zeros(position.shape, F32)
        for edge in (first[1], first[2], total):
            marks = marks + one_if(position >= edge * BLOCK)
        return marks

    for i, start in enumerate(WINDOWS):
        place_in = count((2 * CAP, 1), 0)
        row_image = image_of(place_in - CAP * one_if(place_in >= CAP) + i * CAP)
        key_image = image_of(count((1, 2 * CAP), 1) + start)
        allowed = (row_image == key_image) & (row_image < IMG)
        query = two_heads(qkv[0, i * CAP : (i + 1) * CAP, :])
        scores = dot(query, qkv[1, start : start + 2 * CAP, :], 1, 1) * 0.125
        scores = jnp.where(allowed, scores, -1e30)
        peak = jnp.max(scores, axis=-1, keepdims=True)
        weights = jnp.where(allowed, jnp.exp(scores - peak), 0.0)
        totals = jnp.sum(weights, axis=-1, keepdims=True)
        totals = jnp.where(row_image < IMG, totals, 1.0)
        share = weights / totals
        shares[i] = share
        mixed = dot(share.astype(BF16), qkv[2, start : start + 2 * CAP, :])
        att[i * CAP : (i + 1) * CAP, :] = one_head(mixed).astype(BF16)

    attx[...] = dot(move[...], att[...], 0, 0).astype(BF16)
    pa[c, z] = attx[ROWS:, :]
    za[0]()

    for k in (1, 7, 2, 6, 3, 5, 4):
        ref = gf.at[yat(-k), pl.ds(ROWS, CAP)]
        copy_to(ref, ref, img_s.at[k], img_r.at[k], tensor=yat(k)).wait_recv()
    cotangent = jnp.concatenate([gf[n] for n in range(NT)], axis=1)
    ga[...] = dot(move[...], dot(cotangent, wo[...], 1, 1).astype(BF16)).astype(BF16)

    gacc[...] = jnp.zeros(gacc.shape, F32)
    for i, start in enumerate(WINDOWS):
        window = slice(start, start + 2 * CAP)
        rows = slice(i * CAP, (i + 1) * CAP)
        share = shares[i]
        pull = two_heads(ga[rows, :])
        query = two_heads(qkv[0, rows, :])
        grad_share = dot(pull, qkv[2, window, :], 1, 1)
        inner = jnp.sum(share * grad_share, axis=-1, keepdims=True)
        grad_score = (0.125 * share * (grad_share - inner)).astype(BF16)
        gcat[rows, 0:NARROW] = one_head(dot(grad_score, qkv[1, window, :])).astype(BF16)
        gacc[0, window, :] += dot(grad_score, query, 0, 0)
        gacc[1, window, :] += dot(share.astype(BF16), pull, 0, 0)
    gcat[:, NARROW : 2 * NARROW] = gacc[0].astype(BF16)
    gcat[:, 2 * NARROW :] = gacc[1].astype(BF16)

    mine = (3 - c, c)
    other = (2 + c, 1 - c)

    def core_msg(s):
        return copy_to(part.at[other[s]], crecv.at[s], core_s.at[s], core_r.at[s], dp=sibling)

    for n in range(NT):
        part[3, n * NARROW : (n + 1) * NARROW, :] = dot(attx[...], gf[n], 0, 0).astype(BF16)
    for n in range(NT):
        grads = dot(tf[n], gcat[...], 0, 0)
        for j in range(3):
            part[j, n * NARROW : (n + 1) * NARROW, :] = grads[
                :, j * NARROW : (j + 1) * NARROW
            ].astype(BF16)
    go(core_msg(0))
    go(core_msg(1))

    for n in range(NT):
        weight = jnp.concatenate([wi[j, n * NARROW : (n + 1) * NARROW, :] for j in range(3)], axis=1)
        pback[n] = dot(gcat[...], weight, 1, 1).astype(BF16)

    def reduce_y(buf, land, which):
        def piece(step, way, half):
            return (
                buf.at[yat(way * (5 - step)), pl.ds(half * HALF, HALF)],
                land.at[step - 1, (way + 1) // 2, pl.ds(half * HALF, HALF)],
                which * 16 + ((step - 1) * 2 + (way + 1) // 2) * 2 + half,
            )

        def msg(step, way, half):
            src, dst, sem = piece(step, way, half)
            return copy_to(src, dst, rs_s.at[sem], rs_r.at[sem], tensor=yat(way))

        def begin():
            for way in (1, -1):
                go(msg(1, way, (1 - way) // 2))

        def move(step):
            for half in range(2):
                for way in (1, -1):
                    if step > 2 or half == (1 - way) // 2:
                        msg(step - 1, way, half).wait_recv()
                        src, _, _ = piece(step, way, half)
                        _, got, _ = piece(step - 1, way, half)
                        src[...] = (src[...].astype(F32) + got[...].astype(F32)).astype(BF16)
                    go(msg(step, way, half))

        def finish(out):
            for half in range(2):
                for way in (1, -1):
                    msg(4, way, half).wait_recv()
            out[...] = (
                buf[t].astype(F32) + land[3, 0].astype(F32) + land[3, 1].astype(F32)
            ).astype(BF16)

        return begin, move, finish

    back = reduce_y(pback, rback, 0)
    outs = reduce_y(pout, rout, 1)
    back[0]()

    def core_sum(s):
        core_msg(s).wait_recv()
        csum[s] = (part[mine[s]].astype(F32) + crecv[s].astype(F32)).astype(BF16)

    def xr_msg(s, k):
        peer = xat(k)
        return copy_to(
            csum.at[s, pl.ds(pl.multiple_of(peer * 256, 256), 256)],
            xrecv.at[s, k - 1],
            xr_s.at[s, k],
            xr_r.at[s, k],
            outer=peer,
        )

    def x_send(s):
        for k in (2, 1, 3):
            go(xr_msg(s, k))

    def x_sum(s):
        for k in (1, 3, 2):
            xr_msg(s, k).wait_recv()
        acc = csum[s, pl.ds(pl.multiple_of(o * 256, 256), 256), :].astype(F32)
        for k in range(3):
            acc = acc + xrecv[s, k].astype(F32)
        tsum[s] = acc.astype(BF16)

    def far_first(m):
        half = lax.div(m + 1, 2)
        return 8 + half * (1 - 2 * lax.rem(m, 2))

    def zr_msg(s, k):
        peer = lax.rem(z + k, NZ)
        return copy_to(
            tsum.at[s, pl.ds(pl.multiple_of(peer * 16, 16), 16)],
            zrecv.at[s, k],
            zr_s.at[s, k],
            zr_r.at[s, k],
            dp=2 * peer + c,
        )

    def z_rows(place_z):
        return pl.ds(pl.multiple_of(o * 256 + place_z * 16, 16), 16)

    def zb_msg(s, k):
        peer = lax.rem(z + k, NZ)
        ref = full.at[mine[s], z_rows(z)]
        return copy_to(ref, ref, zb_s.at[s, k], zb_r.at[s, k], dp=2 * peer + c)

    def each_z(fn):
        def body(m, carry):
            fn(far_first(m))
            return carry

        lax.fori_loop(0, NZ - 1, body, 0)

    def z_send(s):
        each_z(lambda k: zr_msg(s, k).start())

    def z_sum(s):
        each_z(lambda k: zr_msg(s, k).wait_recv())
        acc = tsum[s, pl.ds(pl.multiple_of(z * 16, 16), 16), :].astype(F32)
        for k in range(1, NZ):
            acc = acc + zrecv[s, k].astype(F32)
        full[mine[s], z_rows(z), :] = acc.astype(BF16)
        each_z(lambda k: zb_msg(s, k).start())

    def xb_msg(s, k):
        ref = full.at[mine[s], pl.ds(pl.multiple_of(o * 256, 256), 256)]
        return copy_to(ref, ref, xb_s.at[s, k], xb_r.at[s, k], outer=xat(k))

    def xb_wait(s, k):
        ref = full.at[mine[s], pl.ds(pl.multiple_of(xat(NX - k) * 256, 256), 256)]
        copy_to(ref, ref, xb_s.at[s, k], xb_r.at[s, k], outer=xat(k)).wait_recv()

    def cb_msg(s, k):
        ref = full.at[mine[s], pl.ds(pl.multiple_of(xat(NX - k) * 256, 256), 256)]
        return copy_to(ref, ref, cb_s.at[s, k], cb_r.at[s, k], dp=sibling)

    def cb_wait(s, k):
        ref = full.at[other[s], pl.ds(pl.multiple_of(xat(NX - k) * 256, 256), 256)]
        copy_to(ref, ref, cb_s.at[s, k], cb_r.at[s, k], dp=sibling).wait_recv()

    def z_got(s, k):
        ref = full.at[mine[s], z_rows(lax.rem(z + (NZ - k), NZ))]
        peer = lax.rem(z + k, NZ)
        copy_to(ref, ref, zb_s.at[s, k], zb_r.at[s, k], dp=2 * peer + c).wait_recv()

    def spread_x(s):
        each_z(lambda k: z_got(s, k))
        for k in (2, 1, 3):
            go(xb_msg(s, k))
        go(cb_msg(s, 0))

    def spread_core(s):
        for k in (1, 3, 2):
            xb_wait(s, k)
            go(cb_msg(s, k))

    za[1]()
    core_sum(0)
    x_send(0)
    core_sum(1)
    x_send(1)
    za[2]()
    back[1](2)
    za[3]()
    x_sum(0)
    z_send(0)
    x_sum(1)
    z_send(1)
    za[4]()

    coming = one_if(dest_all == here) * one_if(lane3 != group)
    coming = coming * one_if(lane3 >= group - here) * one_if(lane3 < group - here + NDP)
    in_len = jnp.sum(jnp.sum(coming * blocks_all, axis=1, keepdims=True), axis=0, keepdims=True)
    source = jnp.sum(
        jnp.sum(coming * (lane3 - group + here), axis=1, keepdims=True), axis=0, keepdims=True
    )
    put_row, put_col = count((ROWS, CAP), 0), count((ROWS, CAP), 1)
    put = one_if(put_row == put_col + BLOCK * kept_total) * one_if(put_col < BLOCK * in_len)
    incoming = dot(put.astype(BF16), pick(pa, source))
    att[...] = (attx[:ROWS, :].astype(F32) + incoming).astype(BF16)
    for n in range(NT):
        pout[n] = dot(att[...], wo[:, n * NARROW : (n + 1) * NARROW]).astype(BF16)
    outs[0]()
    back[1](3)
    outs[1](2)
    back[1](4)
    z_sum(0)
    z_sum(1)
    outs[1](3)
    back[2](gtok_o)
    outs[1](4)
    spread_x(0)
    spread_x(1)
    outs[2](lay_o)
    spread_core(0)
    spread_core(1)
    for s in range(2):
        for k in (0, 1, 3, 2):
            cb_wait(s, k)
    giw_o[...] = full[0:3]
    for n in range(NT):
        gow_o[:, n * NARROW : (n + 1) * NARROW] = full[3, n * NARROW : (n + 1) * NARROW, :]

    for cp in pending:
        cp.wait_send()
    for s in range(2):
        each_z(lambda k: zr_msg(s, k).wait_send())
        each_z(lambda k: zb_msg(s, k).wait_send())


def on_device(tokens, input_weight, output_weight, grad_layer, patch_blocks, target_group):
    vmem = pl.BlockSpec(memory_space=pltpu.VMEM)
    dma = pltpu.SemaphoreType.DMA

    def buf(*shape, dtype=BF16):
        return pltpu.VMEM(shape, dtype)

    layer_out, grad_tokens, input_sum, output_sum = pl.pallas_call(
        kernel,
        out_shape=(
            jax.ShapeDtypeStruct((ROWS, NARROW), BF16),
            jax.ShapeDtypeStruct((ROWS, NARROW), BF16),
            jax.ShapeDtypeStruct((3, NT * NARROW, NARROW), BF16),
            jax.ShapeDtypeStruct((NARROW, NT * NARROW), BF16),
        ),
        in_specs=[vmem] * 6,
        out_specs=(vmem,) * 4,
        scratch_shapes=[
            buf(NT, ROWS, NARROW),
            buf(NT, EXTRA, NARROW),
            buf(2, NZ, CAP, NARROW),
            buf(2, NZ, CAP, NARROW),
            buf(ROWS, EXTRA),
            buf(3, ROWS, NARROW),
            buf(ROWS, NARROW),
            buf(3, 2 * CAP, 2 * CAP, dtype=F32),
            buf(ROWS, NARROW),
            buf(EXTRA, NARROW),
            buf(ROWS, 3 * NARROW),
            buf(2, ROWS, NARROW, dtype=F32),
            buf(4, 1024, NARROW),
            buf(2, 1024, NARROW),
            buf(2, 1024, NARROW),
            buf(2, 3, 256, NARROW),
            buf(2, 256, NARROW),
            buf(2, NZ, 16, NARROW),
            buf(4, 1024, NARROW),
            buf(NT, ROWS, NARROW),
            buf(NT, ROWS, NARROW),
            buf(4, 2, ROWS, NARROW),
            buf(4, 2, ROWS, NARROW),
            dma((32,)), dma((32,)),
            dma((NT,)), dma((NT,)),
            dma((NZ + 1,)), dma((NZ + 1,)),
            dma((NZ + 1,)), dma((NZ + 1,)),
            dma((2,)), dma((2,)),
            dma((2,)), dma((2,)),
            dma((2, NX)), dma((2, NX)),
            dma((2, NZ)), dma((2, NZ)),
            dma((2, NZ)), dma((2, NZ)),
            dma((2, NX)), dma((2, NX)),
            dma((2, NX)), dma((2, NX)),
            dma((32,)), dma((32,)),
        ],
        compiler_params=pltpu.CompilerParams(
            collective_id=0, has_side_effects=True, vmem_limit_bytes=56 * 2**20
        ),
    )(
        tokens,
        jnp.transpose(input_weight, (1, 0, 2)),
        output_weight,
        grad_layer,
        patch_blocks.T,
        target_group.T,
    )
    grad_input_weight = jnp.transpose(input_sum, (1, 0, 2)).astype(F32)
    return layer_out, grad_tokens, grad_input_weight, output_sum.astype(F32)


def solution(mesh):
    return jax.shard_map(
        on_device,
        mesh=mesh,
        in_specs=(
            P(("outer", "dp"), "tensor"),
            P(None, None, "tensor"),
            P("tensor", None),
            P(("outer", "dp"), "tensor"),
            P(),
            P(),
        ),
        out_specs=(
            P(("outer", "dp"), "tensor"),
            P(("outer", "dp"), "tensor"),
            P(None, None, "tensor"),
            P("tensor", None),
        ),
        check_vma=False,
    )
```

time: 582 us -> 107 us (0.18)
  waiting for transfers between devices: 418 us -> 0 us
  Pallas kernels: 0 us -> 102 us
  blocking collectives: 46.7 us -> 0 us
  starting transfers between devices: 39.6 us -> 0 us
  local copies, waits for them, and re-layouts: 29.3 us -> 1.29 us
  between operations: 21.4 us -> 0.67 us
  other arithmetic: 19 us -> 3.27 us
  matrix products: 7.2 us -> 0 us
    psum x1 -> x0, waiting for transfers between devices: 316 us -> none  [on_device(): lax.psum((term_input, term_output), ('outer', 'dp'))]
    pallas_call x0 -> x1, Pallas kernels: none -> 102 us  [on_device(): pl.pallas_call(kernel, out_shape=(jax.ShapeDtypeStruct((ROWS, NARROW), BF...]
    unnamed x5 -> x0, waiting for transfers between devices: 68.8 us -> none
    all_gather x2 -> x0, blocking collectives: 46.7 us -> none  [the longest x1 24.1 us: on_device(): lax.all_gather(grad_layer, 'tensor', axis=1, tiled=True)]
    all_to_all x2 -> x0, starting transfers between devices: 39.4 us -> none  [the longest x1 20.6 us: on_device(): lax.all_to_all(parcel, 'dp', split_axis=0, concat_axis=0, tiled=True)]
    all_to_all x2 -> x0, waiting for transfers between devices: 33.7 us -> none  [the longest x1 21.9 us: on_device(): lax.all_to_all(parcel, 'dp', split_axis=0, concat_axis=0, tiled=True)]
    gather x11 -> x0, local copies, waits for them, and re-layouts: 14.5 us -> none  [the longest x2 4.25 us: on_device(): jnp.take(padded_proj, block_index, axis=0)]
    unnamed x37 -> x8, local copies, waits for them, and re-layouts: 11 us -> 1.29 us
  transfers between devices with their start and end apart: 5 -> 0, of which waited for: 5 -> 0; matrix products, arithmetic and copies ran while one was open for 3% -> 0% of each run, Pallas kernels for 0% -> 0%
where the time goes in v1:
time: 107 us
  Pallas kernels  102 us (95%)
  other arithmetic  3.27 us (3%)
  local copies, waits for them, and re-layouts  1.29 us (1%)
    pallas_call x1, Pallas kernels, on_device(): pl.pallas_call(kernel, out_shape=(jax.ShapeDtypeStruct((ROWS, NARROW), BF...  102 us
    convert_element_type x1, other arithmetic, on_device(): grad_input_weight = jnp.transpose(input_sum, (1, 0, 2)).astype(F32)  2.43 us

profile of v1, /device:TPU:1, one launch (start us, length us, event | category | flops | bytes accessed | tf_op | source)
XLA Modules:
  0.0 106.8 jit_solution(6721744049118792526)
XLA Ops:
  0.6 101.5 %shard_map.93 = (bf16[384,128]{1,0:T(8,128)(2,1)}, bf16[384,128]{1,0:T(8,128)(2,1)}, bf16[3,1024,128]{2,1,0:T(8,128)(2,1)}, bf16[128,1024]{1,0:T(8,128)(2,1)}) custom-call(bf16[384,128]{1,0:T(8,128)(2,1)} %tok.1, bf16[3,1024,128]{2,1,0:T(8,128)(2,1)} %bitcast.5, bf16[128,1024]{1,0:T(8,128)(2,1)} %wo.1, bf16[384,128]{1,0:T(8,128)(2,1)} %gl.1, ...), custom_call_target="tpu_custom_call" | custom-call | tf_op jit(solution)/shard_map/pallas_call | solution.py:521
  102.2 0.0 copy-start
  102.2 0.0 copy-start.2
  102.2 0.0 copy-start.1
  102.2 2.4 %convert_bitcast_fusion = f32[1024,3,128]{2,0,1:T(8,128)} fusion(bf16[3,1024,128]{2,1,0:T(8,128)(2,1)} %get-tuple-element.10), kind=kLoop, calls=%fused_computation | loop fusion | flops 393216 | bytes 2359296 | tf_op jit(solution)/shard_map/convert_element_type | solution.py:579
  104.6 0.0 copy-done
  104.6 0.8 convert_element_type.11
  105.5 0.0 copy-done.2
  105.5 0.6 copy.12
  106.1 0.0 copy-done.1
  106.1 0.6 copy.13
Async XLA Ops:
  102.2 2.5 %copy-start = (bf16[128,1024]{1,0:T(8,128)(2,1)S(1)}, bf16[128,1024]{1,0:T(8,128)(2,1)}, u32[]{:S(2)}) copy-start(bf16[128,1024]{1,0:T(8,128)(2,1)} %get-tuple-element.11) | copy-start | bytes 786436
  102.2 3.3 %copy-start.2 = (bf16[384,128]{1,0:T(8,128)(2,1)S(1)}, bf16[384,128]{1,0:T(8,128)(2,1)}, u32[]{:S(2)}) copy-start(bf16[384,128]{1,0:T(8,128)(2,1)} %get-tuple-element.16) | copy-start | bytes 294916
  102.2 3.9 %copy-start.1 = (bf16[384,128]{1,0:T(8,128)(2,1)S(1)}, bf16[384,128]{1,0:T(8,128)(2,1)}, u32[]{:S(2)}) copy-start(bf16[384,128]{1,0:T(8,128)(2,1)} %get-tuple-element.17) | copy-start | bytes 294916

commit v2 on v1

--- a/solution.py
+++ b/solution.py
@@ -19,6 +19,7 @@
 NZ = 16
 NX = 4
 NDP = 32
+NEAR = 4
 HALF = ROWS // 2
 EXTRA = ROWS + CAP
 WINDOWS = (0, 64, 128)
@@ -48,13 +49,13 @@
 
 
 def kernel(
-    tok, wi, wo, gl, pb, tg,
-    lay_o, gtok_o, giw_o, gow_o,
-    tf, gf, pg, pa, move, qkv, ga, shares, att, attx, gcat, gacc,
-    part, csum, crecv, xrecv, tsum, zrecv, full,
+    tok, wi_hbm, wo_hbm, gl, pb, tg,
+    lay_o, gtok_o, sum_o,
+    wi, wo, tf, tft, gf, pg, pa, give, got, move, qkv, ga, gax, shares, att, attx, gcat, gacc, gowacc,
+    lay, gtok, part, csum, crecv, xrecv, tsum, zrecv, full,
     pback, pout, rback, rout,
     ring_s, ring_r, img_s, img_r, zg_s, zg_r, za_s, za_r, sib_s, sib_r,
-    core_s, core_r, xr_s, xr_r, zr_s, zr_r, zb_s, zb_r, xb_s, xb_r, cb_s, cb_r,
+    load, store, core_s, core_r, xr_s, xr_r, zr_s, zr_r, zb_s, zb_r, xb_s, xb_r, cb_s, cb_r,
     rs_s, rs_r,
 ):
     o = lax.axis_index("outer")
@@ -79,13 +80,23 @@
         cp.start()
         pending.append(cp)
 
+    loads = [
+        pltpu.make_async_copy(gl, gf.at[t, pl.ds(0, ROWS)], load.at[0]),
+        pltpu.make_async_copy(tok, tf.at[t], load.at[1]),
+        pltpu.make_async_copy(wi_hbm, wi, load.at[2]),
+        pltpu.make_async_copy(wo_hbm, wo, load.at[3]),
+    ]
+    for cp in loads:
+        cp.start()
+
     barrier = pltpu.get_barrier_semaphore()
 
     def greet(**device):
         pl.semaphore_signal(barrier, inc=1, device_id=device, device_id_type=MESH)
 
-    for k in range(1, NZ):
+    for k in range(1, NEAR + 1):
         greet(dp=2 * zat(k) + c)
+        greet(dp=2 * zat(-k) + c)
     greet(dp=sibling)
     for k in range(1, NT):
         greet(tensor=yat(k))
@@ -93,13 +104,30 @@
         greet(outer=xat(k))
 
     here = d.astype(F32)
-    group = (o * NDP + d).astype(F32)
+    beside = sibling.astype(F32)
     lane3 = count((IMG, NARROW), 1)
     blocks_all = pb[...].astype(F32)
     dest_all = tg[...].astype(F32)
-    own = one_if(lane3 == group)
-    length3 = jnp.sum(blocks_all * own, axis=1, keepdims=True)
-    dest3 = jnp.sum(dest_all * own, axis=1, keepdims=True)
+
+    def own_of(table, owner):
+        mark = one_if(lane3 == (o * NDP).astype(F32) + owner)
+        return jnp.sum(table * mark, axis=1, keepdims=True)
+
+    def target_of(owner):
+        takers = own_of(dest_all, owner)
+        return jnp.sum(takers * one_if(takers != owner), axis=0, keepdims=True)
+
+    def coming_to(owner):
+        base = (o * NDP).astype(F32)
+        mark = one_if(dest_all == owner) * one_if(lane3 != base + owner)
+        return mark * one_if(lane3 >= base) * one_if(lane3 < base + NDP)
+
+    def source_of(owner):
+        marks = coming_to(owner) * (lane3 - (o * NDP).astype(F32))
+        return jnp.sum(jnp.sum(marks, axis=1, keepdims=True), axis=0, keepdims=True)
+
+    length3 = own_of(blocks_all, here)
+    dest3 = own_of(dest_all, here)
     length = [length3[i : i + 1] for i in range(IMG)]
     dest = [dest3[i : i + 1] for i in range(IMG)]
     first = [jnp.zeros((1, 1), F32), length[0], length[0] + length[1]]
@@ -109,67 +137,68 @@
     kept = [stays[i] * length[i] for i in range(IMG)]
     place = [jnp.zeros((1, 1), F32), kept[0], kept[0] + kept[1]]
     kept_total = place[2] + kept[2]
-    target = moved[0] * dest[0] + moved[1] * dest[1] + moved[2] * dest[2]
 
     cut = one_if(count((CAP, ROWS), 1) == count((CAP, ROWS), 0) + BLOCK * kept_total)
-    pg[c, z] = dot(cut.astype(BF16), gl[...]).astype(BF16)
-    tf[t] = tok[...]
-    gf[t, :ROWS, :] = gl[...]
-
-    pl.semaphore_wait(barrier, (NZ - 1) + 1 + (NT - 1) + (NX - 1))
+    cut = cut.astype(BF16)
+    loads[0].wait()
+    pg[z] = dot(cut, gf[t, :ROWS, :]).astype(BF16)
+    loads[1].wait()
+
+    pl.semaphore_wait(barrier, 2 * NEAR + 1 + (NT - 1) + (NX - 1))
 
     def gather_z(buf, ss, rs, n):
         def msg(a, j, half=None):
             k = (a + j) % NZ
             sem = NZ if half == 1 else k
-            ref = buf.at[c, zat(-a)]
+            ref = buf.at[zat(-a)]
             if half is not None:
                 ref = ref.at[pl.ds(half * BLOCK, BLOCK)]
             return copy_to(ref, ref, ss.at[sem], rs.at[sem], dp=2 * zat(j) + c)
 
         def arrived(k, half=None):
             sem = NZ if half == 1 else k
-            ref = buf.at[c, zat(-k)]
+            ref = buf.at[zat(-k)]
             if half is not None:
                 ref = ref.at[pl.ds(half * BLOCK, BLOCK)]
             copy_to(ref, ref, ss.at[sem], rs.at[sem], dp=2 * zat(k) + c).wait_recv()
 
         def one():
-            for j in (6, -6, 3, -3, 1, -1):
+            for j in (4, -4, 2, -2, 1, -1):
                 go(msg(0, j))
 
         def two():
-            arrived(3)
-            go(msg(3, 1))
-            go(msg(3, -1))
-            arrived(13)
-            go(msg(-3, -1))
-            go(msg(-3, 1))
-
-        def three():
-            arrived(6)
-            go(msg(6, 2, 0))
-            go(msg(6, 1))
-            go(msg(6, -1))
-            arrived(10)
-            go(msg(-6, -2, 1))
-            go(msg(-6, -1))
-            go(msg(-6, 1))
+            arrived(4)
+            go(msg(4, 4, 0))
+            arrived(12)
+            go(msg(-4, -4, 1))
+            for j in (3, 2, 1, -1):
+                go(msg(4, j))
+                go(msg(-4, -j))
 
         def cross():
-            return copy_to(buf.at[c], buf.at[c], sib_s.at[n], sib_r.at[n], dp=sibling)
-
-        def four():
-            for k in (1, 15, 2, 14, 4, 12, 5, 11, 7, 9):
+            return copy_to(give.at[n], got.at[n], sib_s.at[n], sib_r.at[n], dp=sibling)
+
+        def pick(peer):
+            acc = jnp.zeros((CAP, NARROW), BF16)
+            for k in range(NZ):
+                mark = one_if(peer == (c + 2 * k).astype(F32))
+                acc = acc + buf[k] * jnp.broadcast_to(mark, (1, NARROW)).astype(BF16)
+            return acc
+
+        def three(other_peer):
+            for k in (1, 15, 2, 14, 3, 13, 5, 11, 6, 10, 7, 9):
                 arrived(k)
             arrived(8, 0)
             arrived(8, 1)
+            give[n] = pick(other_peer)
             go(cross())
 
-        def five():
+        def four(peer):
+            acc = pick(peer)
             cross().wait_recv()
-
-        return one, two, three, four, five
+            return acc + got[n]
+
+        return one, two, three, four
 
     zg = gather_z(pg, zg_s, zg_r, 0)
     za = gather_z(pa, za_s, za_r, 1)
@@ -205,25 +234,18 @@
     ring_sends(1)
     zg[1]()
     ring_waits(1)
-    zg[2]()
     ring_waits(2)
-    zg[3]()
-    zg[4]()
-
-    def pick(buf, peer):
-        acc = jnp.zeros((CAP, NARROW), BF16)
-        for k in range(NDP):
-            mark = jnp.broadcast_to(one_if(peer == float(k)), (1, NARROW)).astype(BF16)
-            acc = acc + buf[k % 2, k // 2] * mark
-        return acc
-
-    gf[t, ROWS:, :] = pick(pg, target)
+    zg[2](target_of(beside))
+
+    gf[t, ROWS:, :] = zg[3](target_of(here))
     img_ref = gf.at[t, pl.ds(ROWS, CAP)]
     for k in (4, 3, 5, 2, 6, 1, 7):
         go(copy_to(img_ref, img_ref, img_s.at[k], img_r.at[k], tensor=yat(k)))
     ring_waits(3)
     ring_waits(4)
 
+    loads[2].wait()
+    loads[3].wait()
     tokens = jnp.concatenate([tf[n] for n in range(NT)], axis=1)
     for j in range(3):
         qkv[j] = dot(tokens, wi[j]).astype(BF16)
@@ -273,14 +295,22 @@
         att[i * CAP : (i + 1) * CAP, :] = one_head(mixed).astype(BF16)
 
     attx[...] = dot(move[...], att[...], 0, 0).astype(BF16)
-    pa[c, z] = attx[ROWS:, :]
+    pa[z] = attx[ROWS:, :]
     za[0]()
+
+    for n in range(NT):
+        tft[n] = tf[n].T
+    cotangent = jnp.concatenate([gf[n, :ROWS, :] for n in range(NT)], axis=1)
+    gax[:ROWS, :] = dot(cotangent, wo[...], 1, 1).astype(BF16)
+    for n in range(NT):
+        gowacc[n] = dot(attx[:ROWS, :], gf[n, :ROWS, :], 0, 0)
 
     for k in (1, 7, 2, 6, 3, 5, 4):
         ref = gf.at[yat(-k), pl.ds(ROWS, CAP)]
         copy_to(ref, ref, img_s.at[k], img_r.at[k], tensor=yat(k)).wait_recv()
-    cotangent = jnp.concatenate([gf[n] for n in range(NT)], axis=1)
-    ga[...] = dot(move[...], dot(cotangent, wo[...], 1, 1).astype(BF16)).astype(BF16)
+    cotangent = jnp.concatenate([gf[n, ROWS:, :] for n in range(NT)], axis=1)
+    gax[ROWS:, :] = dot(cotangent, wo[...], 1, 1).astype(BF16)
+    ga[...] = dot(move[...], gax[...]).astype(BF16)
 
     gacc[...] = jnp.zeros(gacc.shape, F32)
     for i, start in enumerate(WINDOWS):
@@ -305,19 +335,16 @@
         return copy_to(part.at[other[s]], crecv.at[s], core_s.at[s], core_r.at[s], dp=sibling)
 
     for n in range(NT):
-        part[3, n * NARROW : (n + 1) * NARROW, :] = dot(attx[...], gf[n], 0, 0).astype(BF16)
+        rows = slice(n * NARROW, (n + 1) * NARROW)
+        part[2, rows, :] = dot(tft[n], gcat[:, 2 * NARROW :]).astype(BF16)
+        part[3, rows, :] = (gowacc[n] + dot(attx[ROWS:, :], gf[n, ROWS:, :], 0, 0)).astype(BF16)
+    go(core_msg(0))
     for n in range(NT):
-        grads = dot(tf[n], gcat[...], 0, 0)
-        for j in range(3):
-            part[j, n * NARROW : (n + 1) * NARROW, :] = grads[
-                :, j * NARROW : (j + 1) * NARROW
-            ].astype(BF16)
-    go(core_msg(0))
+        rows = slice(n * NARROW, (n + 1) * NARROW)
+        grads = dot(tft[n], gcat[:, : 2 * NARROW])
+        part[0, rows, :] = grads[:, :NARROW].astype(BF16)
+        part[1, rows, :] = grads[:, NARROW:].astype(BF16)
     go(core_msg(1))
-
-    for n in range(NT):
-        weight = jnp.concatenate([wi[j, n * NARROW : (n + 1) * NARROW, :] for j in range(3)], axis=1)
-        pback[n] = dot(gcat[...], weight, 1, 1).astype(BF16)
 
     def reduce_y(buf, land, which):
         def piece(step, way, half):
@@ -357,7 +384,6 @@
 
     back = reduce_y(pback, rback, 0)
     outs = reduce_y(pout, rout, 1)
-    back[0]()
 
     def core_sum(s):
         core_msg(s).wait_recv()
@@ -457,90 +483,139 @@
             xb_wait(s, k)
             go(cb_msg(s, k))
 
-    za[1]()
     core_sum(0)
     x_send(0)
     core_sum(1)
     x_send(1)
-    za[2]()
-    back[1](2)
-    za[3]()
+    za[1]()
+
+    for n in range(NT):
+        weight = jnp.concatenate([wi[j, n * NARROW : (n + 1) * NARROW, :] for j in range(3)], axis=1)
+        pback[n] = dot(gcat[...], weight, 1, 1).astype(BF16)
+    back[0]()
     x_sum(0)
     z_send(0)
     x_sum(1)
     z_send(1)
-    za[4]()
-
-    coming = one_if(dest_all == here) * one_if(lane3 != group)
-    coming = coming * one_if(lane3 >= group - here) * one_if(lane3 < group - here + NDP)
-    in_len = jnp.sum(jnp.sum(coming * blocks_all, axis=1, keepdims=True), axis=0, keepdims=True)
-    source = jnp.sum(
-        jnp.sum(coming * (lane3 - group + here), axis=1, keepdims=True), axis=0, keepdims=True
+    za[2](source_of(beside))
+    back[1](2)
+
+    in_len = jnp.sum(
+        jnp.sum(coming_to(here) * blocks_all, axis=1, keepdims=True), axis=0, keepdims=True
     )
     put_row, put_col = count((ROWS, CAP), 0), count((ROWS, CAP), 1)
     put = one_if(put_row == put_col + BLOCK * kept_total) * one_if(put_col < BLOCK * in_len)
-    incoming = dot(put.astype(BF16), pick(pa, source))
+    incoming = dot(put.astype(BF16), za[3](source_of(here)))
     att[...] = (attx[:ROWS, :].astype(F32) + incoming).astype(BF16)
     for n in range(NT):
         pout[n] = dot(att[...], wo[:, n * NARROW : (n + 1) * NARROW]).astype(BF16)
     outs[0]()
     back[1](3)
+    z_sum(0)
+    z_sum(1)
     outs[1](2)
     back[1](4)
-    z_sum(0)
-    z_sum(1)
     outs[1](3)
-    back[2](gtok_o)
-    outs[1](4)
+    stores = []
+
+    def keep(src, dst):
+        cp = pltpu.make_async_copy(src, dst, store.at[len(stores)])
+        cp.start()
+        stores.append(cp)
+
+    def keep_piece(chunk, k):
+        rows = pl.ds(pl.multiple_of(xat(NX - k) * 256, 256), 256)
+        keep(full.at[chunk, rows], sum_o.at[chunk, rows])
+
+    back[2](gtok)
+    keep(gtok, gtok_o)
     spread_x(0)
     spread_x(1)
-    outs[2](lay_o)
-    spread_core(0)
-    spread_core(1)
+    outs[1](4)
+    for s in range(2):
+        spread_core(s)
+        for k in range(NX):
+            keep_piece(mine[s], k)
+    outs[2](lay)
+    keep(lay, lay_o)
     for s in range(2):
         for k in (0, 1, 3, 2):
             cb_wait(s, k)
-    giw_o[...] = full[0:3]
-    for n in range(NT):
-        gow_o[:, n * NARROW : (n + 1) * NARROW] = full[3, n * NARROW : (n + 1) * NARROW, :]
+            keep_piece(other[s], k)
 
     for cp in pending:
         cp.wait_send()
     for s in range(2):
         each_z(lambda k: zr_msg(s, k).wait_send())
         each_z(lambda k: zb_msg(s, k).wait_send())
+    for cp in stores:
+        cp.wait()
+
+
+def finish(
+    lay_i, gtok_i, sum_i, lay_o, gtok_o, giw_o, gow_o, low, wide, flat, lay, gtok, sem_i, sem_o
+):
+    reads = [pltpu.make_async_copy(sum_i.at[j], low.at[j], sem_i.at[j]) for j in range(4)]
+    reads.append(pltpu.make_async_copy(lay_i, lay, sem_i.at[4]))
+    reads.append(pltpu.make_async_copy(gtok_i, gtok, sem_i.at[5]))
+    copies = []
+    for cp in reads:
+        cp.start()
+    for j in range(3):
+        reads[j].wait()
+        wide[j] = low[j].astype(F32)
+        copies.append(pltpu.make_async_copy(wide.at[j], giw_o.at[j], sem_o.at[j]))
+        copies[-1].start()
+    reads[3].wait()
+    for n in range(NT):
+        columns = slice(n * NARROW, (n + 1) * NARROW)
+        flat[:, columns] = low[3, columns, :].astype(F32)
+    copies.append(pltpu.make_async_copy(flat, gow_o, sem_o.at[3]))
+    copies[-1].start()
+    for j, src, dst in ((4, lay, lay_o), (5, gtok, gtok_o)):
+        reads[j].wait()
+        copies.append(pltpu.make_async_copy(src, dst, sem_o.at[j]))
+        copies[-1].start()
+    for cp in copies:
+        cp.wait()
 
 
 def on_device(tokens, input_weight, output_weight, grad_layer, patch_blocks, target_group):
     vmem = pl.BlockSpec(memory_space=pltpu.VMEM)
+    hbm = pl.BlockSpec(memory_space=pl.ANY)
     dma = pltpu.SemaphoreType.DMA
 
     def buf(*shape, dtype=BF16):
         return pltpu.VMEM(shape, dtype)
 
-    layer_out, grad_tokens, input_sum, output_sum = pl.pallas_call(
+    rows_bf16 = jax.ShapeDtypeStruct((ROWS, NARROW), BF16)
+    layer_out, grad_tokens, sums = pl.pallas_call(
         kernel,
-        out_shape=(
-            jax.ShapeDtypeStruct((ROWS, NARROW), BF16),
-            jax.ShapeDtypeStruct((ROWS, NARROW), BF16),
-            jax.ShapeDtypeStruct((3, NT * NARROW, NARROW), BF16),
-            jax.ShapeDtypeStruct((NARROW, NT * NARROW), BF16),
-        ),
-        in_specs=[vmem] * 6,
-        out_specs=(vmem,) * 4,
+        out_shape=(rows_bf16, rows_bf16, jax.ShapeDtypeStruct((4, NT * NARROW, NARROW), BF16)),
+        in_specs=[hbm] * 4 + [vmem] * 2,
+        out_specs=(hbm,) * 3,
         scratch_shapes=[
+            buf(3, 1024, NARROW),
+            buf(NARROW, 1024),
             buf(NT, ROWS, NARROW),
+            buf(NT, NARROW, ROWS),
             buf(NT, EXTRA, NARROW),
-            buf(2, NZ, CAP, NARROW),
-            buf(2, NZ, CAP, NARROW),
+            buf(NZ, CAP, NARROW),
+            buf(NZ, CAP, NARROW),
+            buf(2, CAP, NARROW),
+            buf(2, CAP, NARROW),
             buf(ROWS, EXTRA),
             buf(3, ROWS, NARROW),
             buf(ROWS, NARROW),
+            buf(EXTRA, NARROW),
             buf(3, 2 * CAP, 2 * CAP, dtype=F32),
             buf(ROWS, NARROW),
             buf(EXTRA, NARROW),
             buf(ROWS, 3 * NARROW),
             buf(2, ROWS, NARROW, dtype=F32),
+            buf(NT, NARROW, NARROW, dtype=F32),
+            buf(ROWS, NARROW),
+            buf(ROWS, NARROW),
             buf(4, 1024, NARROW),
             buf(2, 1024, NARROW),
             buf(2, 1024, NARROW),
@@ -557,6 +632,7 @@
             dma((NZ + 1,)), dma((NZ + 1,)),
             dma((NZ + 1,)), dma((NZ + 1,)),
             dma((2,)), dma((2,)),
+            dma((4,)), dma((18,)),
             dma((2,)), dma((2,)),
             dma((2, NX)), dma((2, NX)),
             dma((2, NZ)), dma((2, NZ)),
@@ -576,8 +652,28 @@
         patch_blocks.T,
         target_group.T,
     )
-    grad_input_weight = jnp.transpose(input_sum, (1, 0, 2)).astype(F32)
-    return layer_out, grad_tokens, grad_input_weight, output_sum.astype(F32)
+    layer_out, grad_tokens, input_sum, output_sum = pl.pallas_call(
+        finish,
+        out_shape=(
+            rows_bf16,
+            rows_bf16,
+            jax.ShapeDtypeStruct((3, NT * NARROW, NARROW), F32),
+            jax.ShapeDtypeStruct((NARROW, NT * NARROW), F32),
+        ),
+        in_specs=[hbm] * 3,
+        out_specs=(hbm,) * 4,
+        scratch_shapes=[
+            buf(4, NT * NARROW, NARROW),
+            buf(3, NT * NARROW, NARROW, dtype=F32),
+            buf(NARROW, NT * NARROW, dtype=F32),
+            buf(ROWS, NARROW),
+            buf(ROWS, NARROW),
+            dma((6,)),
+            dma((6,)),
+        ],
+        compiler_params=pltpu.CompilerParams(vmem_limit_bytes=56 * 2**20),
+    )(layer_out, grad_tokens, sums)
+    return layer_out, grad_tokens, jnp.transpose(input_sum, (1, 0, 2)), output_sum
 
 
 def solution(mesh):

time: 107 us -> 96.7 us (0.904)
  Pallas kernels: 102 us -> 95.8 us
  other arithmetic: 3.27 us -> 0 us
  local copies, waits for them, and re-layouts: 1.29 us -> 0 us
    pallas_call x1 -> x2, Pallas kernels: 102 us -> 95.8 us  [the longest x1 93.4 us: on_device(): pl.pallas_call(kernel, out_shape=(rows_bf16, rows_bf16, jax.ShapeDtypeStr...]
    convert_element_type x2 -> x0, other arithmetic: 3.27 us -> none  [the longest x1 2.43 us: on_device(): grad_input_weight = jnp.transpose(input_sum, (1, 0, 2)).astype(F32)]
    unnamed x8 -> x0, local copies, waits for them, and re-layouts: 1.29 us -> none
where the time goes in v2:
time: 96.7 us; the launch traced here: 96.5 us
  Pallas kernels  95.8 us (99%)
    pallas_call x1, Pallas kernels, on_device(): pl.pallas_call(kernel, out_shape=(rows_bf16, rows_bf16, jax.ShapeDtypeStr...  93.4 us
    pallas_call x1, Pallas kernels, on_device(): pl.pallas_call(finish, out_shape=(rows_bf16, rows_bf16, jax.ShapeDtypeStr...  2.45 us

profile of v2, /device:TPU:1, one launch (start us, length us, event | category | flops | bytes accessed | tf_op | source)
XLA Modules:
  0.0 96.5 jit_solution(16458264926543248326)
XLA Ops:
  0.6 93.4 %shard_map.93 = (bf16[384,128]{1,0:T(8,128)(2,1)}, bf16[384,128]{1,0:T(8,128)(2,1)}, bf16[4,1024,128]{2,1,0:T(8,128)(2,1)}) custom-call(bf16[384,128]{1,0:T(8,128)(2,1)} %tok.1, bf16[3,1024,128]{2,1,0:T(8,128)(2,1)} %bitcast.4, bf16[128,1024]{1,0:T(8,128)(2,1)} %wo_hbm.1, bf16[384,128]{1,0:T(8,128)(2,1)} %gl.1, s32[3,128]{1,0:T(4,128)} %bitcast.5, ...), custom_call_target="tpu_custom_call" | custom-call | tf_op jit(solution)/shard_map/pallas_call | solution.py:592
  94.0 2.5 %shard_map.94 = (bf16[384,128]{1,0:T(8,128)(2,1)}, bf16[384,128]{1,0:T(8,128)(2,1)}, f32[3,1024,128]{2,1,0:T(8,128)}, f32[128,1024]{1,0:T(8,128)}) custom-call(bf16[384,128]{1,0:T(8,128)(2,1)} %get-tuple-element.11.lay_i, bf16[384,128]{1,0:T(8,128)(2,1)} %get-tuple-element.12.gtok_i, bf16[4,1024,128]{2,1,0:T(8,128)(2,1)} %get-tuple-element.13.sum_i), custom_call_target="tpu_custom_call" | custom-call | tf_op jit(solution)/shard_map/pallas_call | solution.py:655

commit v3 on v2

--- a/solution.py
+++ b/solution.py
@@ -232,16 +232,16 @@
 
     zg[0]()
     ring_sends(1)
+    ring_waits(1)
     zg[1]()
-    ring_waits(1)
     ring_waits(2)
+    ring_waits(3)
     zg[2](target_of(beside))
 
     gf[t, ROWS:, :] = zg[3](target_of(here))
     img_ref = gf.at[t, pl.ds(ROWS, CAP)]
     for k in (4, 3, 5, 2, 6, 1, 7):
         go(copy_to(img_ref, img_ref, img_s.at[k], img_r.at[k], tensor=yat(k)))
-    ring_waits(3)
     ring_waits(4)
 
     loads[2].wait()
@@ -328,6 +328,8 @@
     gcat[:, NARROW : 2 * NARROW] = gacc[0].astype(BF16)
     gcat[:, 2 * NARROW :] = gacc[1].astype(BF16)
 
+    za[1]()
+
     mine = (3 - c, c)
     other = (2 + c, 1 - c)
 
@@ -347,40 +349,49 @@
     go(core_msg(1))
 
     def reduce_y(buf, land, which):
-        def piece(step, way, half):
-            return (
-                buf.at[yat(way * (5 - step)), pl.ds(half * HALF, HALF)],
-                land.at[step - 1, (way + 1) // 2, pl.ds(half * HALF, HALF)],
-                which * 16 + ((step - 1) * 2 + (way + 1) // 2) * 2 + half,
-            )
-
-        def msg(step, way, half):
-            src, dst, sem = piece(step, way, half)
-            return copy_to(src, dst, rs_s.at[sem], rs_r.at[sem], tensor=yat(way))
+        def plan(kind, way):
+            w = (1 - way) // 2
+            half = pl.ds(w * HALF, HALF)
+            if kind == 0:
+                return buf.at[yat(3 * way)], land.at[w], w, way
+            if kind == 1:
+                return buf.at[yat(4 * way), half], land.at[2, half], 2 + w, 2 * way
+            if kind == 2:
+                return buf.at[yat(way)], land.at[3 + w], 4 + w, way
+            return buf.at[yat(2 * way)], land.at[5 + w], 6 + w, 2 * way
+
+        def msg(kind, way):
+            src, dst, sem, hop = plan(kind, way)
+            sem = which * 8 + sem
+            return copy_to(src, dst, rs_s.at[sem], rs_r.at[sem], tensor=yat(hop))
 
         def begin():
+            for kind in (1, 0, 2):
+                for way in (1, -1):
+                    go(msg(kind, way))
+
+        def middle():
             for way in (1, -1):
-                go(msg(1, way, (1 - way) // 2))
-
-        def move(step):
-            for half in range(2):
+                w = (1 - way) // 2
+                msg(0, way).wait_recv()
+                msg(1, way).wait_recv()
+                for half in range(2):
+                    rows = slice(half * HALF, (half + 1) * HALF)
+                    acc = buf[yat(2 * way), rows, :].astype(F32) + land[w, rows, :].astype(F32)
+                    if half == w:
+                        acc = acc + land[2, rows, :].astype(F32)
+                    buf[yat(2 * way), rows, :] = acc.astype(BF16)
+                go(msg(3, way))
+
+        def last(out):
+            acc = buf[t].astype(F32)
+            for kind in (2, 3):
                 for way in (1, -1):
-                    if step > 2 or half == (1 - way) // 2:
-                        msg(step - 1, way, half).wait_recv()
-                        src, _, _ = piece(step, way, half)
-                        _, got, _ = piece(step - 1, way, half)
-                        src[...] = (src[...].astype(F32) + got[...].astype(F32)).astype(BF16)
-                    go(msg(step, way, half))
-
-        def finish(out):
-            for half in range(2):
-                for way in (1, -1):
-                    msg(4, way, half).wait_recv()
-            out[...] = (
-                buf[t].astype(F32) + land[3, 0].astype(F32) + land[3, 1].astype(F32)
-            ).astype(BF16)
-
-        return begin, move, finish
+                    msg(kind, way).wait_recv()
+                    acc = acc + land[2 * kind - 1 + (1 - way) // 2].astype(F32)
+            out[...] = acc.astype(BF16)
+
+        return begin, middle, last
 
     back = reduce_y(pback, rback, 0)
     outs = reduce_y(pout, rout, 1)
@@ -487,7 +498,6 @@
     x_send(0)
     core_sum(1)
     x_send(1)
-    za[1]()
 
     for n in range(NT):
         weight = jnp.concatenate([wi[j, n * NARROW : (n + 1) * NARROW, :] for j in range(3)], axis=1)
@@ -498,7 +508,7 @@
     x_sum(1)
     z_send(1)
     za[2](source_of(beside))
-    back[1](2)
+    back[1]()
 
     in_len = jnp.sum(
         jnp.sum(coming_to(here) * blocks_all, axis=1, keepdims=True), axis=0, keepdims=True
@@ -510,12 +520,9 @@
     for n in range(NT):
         pout[n] = dot(att[...], wo[:, n * NARROW : (n + 1) * NARROW]).astype(BF16)
     outs[0]()
-    back[1](3)
     z_sum(0)
     z_sum(1)
-    outs[1](2)
-    back[1](4)
-    outs[1](3)
+    outs[1]()
     stores = []
 
     def keep(src, dst):
@@ -531,13 +538,12 @@
     keep(gtok, gtok_o)
     spread_x(0)
     spread_x(1)
-    outs[1](4)
+    outs[2](lay)
+    keep(lay, lay_o)
     for s in range(2):
         spread_core(s)
         for k in range(NX):
             keep_piece(mine[s], k)
-    outs[2](lay)
-    keep(lay, lay_o)
     for s in range(2):
         for k in (0, 1, 3, 2):
             cb_wait(s, k)
@@ -625,8 +631,8 @@
             buf(4, 1024, NARROW),
             buf(NT, ROWS, NARROW),
             buf(NT, ROWS, NARROW),
-            buf(4, 2, ROWS, NARROW),
-            buf(4, 2, ROWS, NARROW),
+            buf(7, ROWS, NARROW),
+            buf(7, ROWS, NARROW),
             dma((32,)), dma((32,)),
             dma((NT,)), dma((NT,)),
             dma((NZ + 1,)), dma((NZ + 1,)),
@@ -639,7 +645,7 @@
             dma((2, NZ)), dma((2, NZ)),
             dma((2, NX)), dma((2, NX)),
             dma((2, NX)), dma((2, NX)),
-            dma((32,)), dma((32,)),
+            dma((16,)), dma((16,)),
         ],
         compiler_params=pltpu.CompilerParams(
             collective_id=0, has_side_effects=True, vmem_limit_bytes=56 * 2**20

time: 96.7 us -> 89.8 us (0.929)
  Pallas kernels: 95.8 us -> 89 us
    pallas_call x1, Pallas kernels: 93.4 us -> 86.5 us  [on_device(): pl.pallas_call(kernel, out_shape=(rows_bf16, rows_bf16, jax.ShapeDtypeStr...]
where the time goes in v3:
time: 89.8 us; the launch traced here: 89.6 us
  Pallas kernels  89 us (99%)
    pallas_call x1, Pallas kernels, on_device(): pl.pallas_call(kernel, out_shape=(rows_bf16, rows_bf16, jax.ShapeDtypeStr...  86.5 us
    pallas_call x1, Pallas kernels, on_device(): pl.pallas_call(finish, out_shape=(rows_bf16, rows_bf16, jax.ShapeDtypeStr...  2.45 us

profile of v3, /device:TPU:1, one launch (start us, length us, event | category | flops | bytes accessed | tf_op | source)
XLA Modules:
  0.0 89.6 jit_solution(13324879825758611485)
XLA Ops:
  0.6 86.5 %shard_map.93 = (bf16[384,128]{1,0:T(8,128)(2,1)}, bf16[384,128]{1,0:T(8,128)(2,1)}, bf16[4,1024,128]{2,1,0:T(8,128)(2,1)}) custom-call(bf16[384,128]{1,0:T(8,128)(2,1)} %tok.1, bf16[3,1024,128]{2,1,0:T(8,128)(2,1)} %bitcast.4, bf16[128,1024]{1,0:T(8,128)(2,1)} %wo_hbm.1, bf16[384,128]{1,0:T(8,128)(2,1)} %gl.1, s32[3,128]{1,0:T(4,128)} %bitcast.5, ...), custom_call_target="tpu_custom_call" | custom-call | tf_op jit(solution)/shard_map/pallas_call | solution.py:598
  87.1 2.5 %shard_map.94 = (bf16[384,128]{1,0:T(8,128)(2,1)}, bf16[384,128]{1,0:T(8,128)(2,1)}, f32[3,1024,128]{2,1,0:T(8,128)}, f32[128,1024]{1,0:T(8,128)}) custom-call(bf16[384,128]{1,0:T(8,128)(2,1)} %get-tuple-element.11.lay_i, bf16[384,128]{1,0:T(8,128)(2,1)} %get-tuple-element.12.gtok_i, bf16[4,1024,128]{2,1,0:T(8,128)(2,1)} %get-tuple-element.13.sum_i), custom_call_target="tpu_custom_call" | custom-call | tf_op jit(solution)/shard_map/pallas_call | solution.py:661

commit v4 on v3

--- a/solution.py
+++ b/solution.py
@@ -51,7 +51,7 @@
 def kernel(
     tok, wi_hbm, wo_hbm, gl, pb, tg,
     lay_o, gtok_o, sum_o,
-    wi, wo, tf, tft, gf, pg, pa, give, got, move, qkv, ga, gax, shares, att, attx, gcat, gacc, gowacc,
+    wi, wo, tf, tft, gf, pg, pa, give, got, move, qkv, ga, gax, shares, att, attx, gcat, gacc, qacc, gaacc, gowacc, wacc, hand, thand, hshare, ghand,
     lay, gtok, part, csum, crecv, xrecv, tsum, zrecv, full,
     pback, pout, rback, rout,
     ring_s, ring_r, img_s, img_r, zg_s, zg_r, za_s, za_r, sib_s, sib_r,
@@ -235,33 +235,6 @@
     ring_waits(1)
     zg[1]()
     ring_waits(2)
-    ring_waits(3)
-    zg[2](target_of(beside))
-
-    gf[t, ROWS:, :] = zg[3](target_of(here))
-    img_ref = gf.at[t, pl.ds(ROWS, CAP)]
-    for k in (4, 3, 5, 2, 6, 1, 7):
-        go(copy_to(img_ref, img_ref, img_s.at[k], img_r.at[k], tensor=yat(k)))
-    ring_waits(4)
-
-    loads[2].wait()
-    loads[3].wait()
-    tokens = jnp.concatenate([tf[n] for n in range(NT)], axis=1)
-    for j in range(3):
-        qkv[j] = dot(tokens, wi[j]).astype(BF16)
-
-    lane = lax.broadcasted_iota(jnp.int32, (1, NARROW), 1)
-    low = lane < BLOCK
-    zero = jnp.zeros((), F32)
-
-    def two_heads(x):
-        x = x.astype(F32)
-        return jnp.concatenate(
-            [jnp.where(low, x, zero).astype(BF16), jnp.where(low, zero, x).astype(BF16)], axis=0
-        )
-
-    def one_head(x):
-        return jnp.where(low, x[:CAP], x[CAP:])
 
     row = count((ROWS, 1), 0)
     column = jnp.full((ROWS, 1), -1.0, F32)
@@ -270,6 +243,58 @@
         shift = BLOCK * (stays[i] * place[i] + moved[i] * BLOCKS - first[i])
         column = column + inside * (row + shift + 1.0)
     move[...] = one_if(count((ROWS, EXTRA), 1) == column).astype(BF16)
+
+    def columns_of(slot):
+        return pl.ds(pl.multiple_of(slot * NARROW, NARROW), NARROW)
+
+    def project(offsets, begin):
+        slots = [yat(k) for k in offsets]
+        shard = jnp.concatenate([tf[slot] for slot in slots], axis=1)
+        weight = jnp.concatenate(
+            [
+                jnp.concatenate([wi[j, columns_of(slot), :] for j in range(3)], axis=1)
+                for slot in slots
+            ],
+            axis=0,
+        )
+        term = dot(shard, weight)
+        qacc[...] = term if begin else qacc[...] + term
+        shard = jnp.concatenate([gf[slot, :ROWS, :] for slot in slots], axis=1)
+        weight = jnp.concatenate([wo[:, columns_of(slot)] for slot in slots], axis=1)
+        term = dot(shard, weight, 1, 1)
+        gaacc[...] = term if begin else gaacc[...] + term
+        for slot in slots:
+            tft[slot] = tf[slot].T
+
+    loads[2].wait()
+    loads[3].wait()
+    project((0, 1, -1, 2, -2), True)
+    ring_waits(3)
+    project((3, -3), False)
+    zg[2](target_of(beside))
+
+    gf[t, ROWS:, :] = zg[3](target_of(here))
+    img_ref = gf.at[t, pl.ds(ROWS, CAP)]
+    for k in (4, 3, 5, 2, 6, 1, 7):
+        go(copy_to(img_ref, img_ref, img_s.at[k], img_r.at[k], tensor=yat(k)))
+    ring_waits(4)
+
+    project((4,), False)
+    for j in range(3):
+        qkv[j] = qacc[:, j * NARROW : (j + 1) * NARROW].astype(BF16)
+
+    lane = lax.broadcasted_iota(jnp.int32, (1, NARROW), 1)
+    low = lane < BLOCK
+    zero = jnp.zeros((), F32)
+
+    def two_heads(x):
+        x = x.astype(F32)
+        return jnp.concatenate(
+            [jnp.where(low, x, zero).astype(BF16), jnp.where(low, zero, x).astype(BF16)], axis=0
+        )
+
+    def one_head(x):
+        return jnp.where(low, x[:CAP], x[CAP:])
 
     def image_of(position):
         marks = jnp.zeros(position.shape, F32)
@@ -298,19 +323,10 @@
     pa[z] = attx[ROWS:, :]
     za[0]()
 
-    for n in range(NT):
-        tft[n] = tf[n].T
-    cotangent = jnp.concatenate([gf[n, :ROWS, :] for n in range(NT)], axis=1)
-    gax[:ROWS, :] = dot(cotangent, wo[...], 1, 1).astype(BF16)
+    gax[...] = gaacc[...].astype(BF16)
     for n in range(NT):
         gowacc[n] = dot(attx[:ROWS, :], gf[n, :ROWS, :], 0, 0)
-
-    for k in (1, 7, 2, 6, 3, 5, 4):
-        ref = gf.at[yat(-k), pl.ds(ROWS, CAP)]
-        copy_to(ref, ref, img_s.at[k], img_r.at[k], tensor=yat(k)).wait_recv()
-    cotangent = jnp.concatenate([gf[n, ROWS:, :] for n in range(NT)], axis=1)
-    gax[ROWS:, :] = dot(cotangent, wo[...], 1, 1).astype(BF16)
-    ga[...] = dot(move[...], gax[...]).astype(BF16)
+    ga[...] = dot(move[:, :ROWS], gax[...]).astype(BF16)
 
     gacc[...] = jnp.zeros(gacc.shape, F32)
     for i, start in enumerate(WINDOWS):
@@ -328,7 +344,39 @@
     gcat[:, NARROW : 2 * NARROW] = gacc[0].astype(BF16)
     gcat[:, 2 * NARROW :] = gacc[1].astype(BF16)
 
-    za[1]()
+    for n in range(NT):
+        grads = dot(tft[n], gcat[...])
+        for j in range(3):
+            wacc[j, n * NARROW : (n + 1) * NARROW, :] = grads[:, j * NARROW : (j + 1) * NARROW]
+
+    lift = move[:, ROWS:]
+    for j in range(3):
+        hand[j] = dot(lift, qkv[j], 0, 0).astype(BF16)
+    for n in range(NT):
+        thand[n] = dot(tft[n], lift).astype(BF16)
+    rows_handed = BLOCK * (moved[0] * length[0] + moved[1] * length[1] + moved[2] * length[2])
+    place_in = count((2 * CAP, 1), 0)
+    row_ok = place_in - CAP * one_if(place_in >= CAP) < rows_handed
+    allowed = row_ok & (count((1, CAP), 1) < rows_handed)
+    scores = dot(two_heads(hand[0]), hand[1], 1, 1) * 0.125
+    scores = jnp.where(allowed, scores, -1e30)
+    weights = jnp.where(allowed, jnp.exp(scores - jnp.max(scores, axis=-1, keepdims=True)), 0.0)
+    totals = jnp.sum(weights, axis=-1, keepdims=True)
+    hshare[...] = weights / jnp.where(row_ok, totals, 1.0)
+
+
+    for k in (1, 7, 2, 6, 3, 5, 4):
+        ref = gf.at[yat(-k), pl.ds(ROWS, CAP)]
+        copy_to(ref, ref, img_s.at[k], img_r.at[k], tensor=yat(k)).wait_recv()
+    cotangent = jnp.concatenate([gf[n, ROWS:, :] for n in range(NT)], axis=1)
+    share = hshare[...]
+    pull = two_heads(dot(cotangent, wo[...], 1, 1).astype(BF16))
+    grad_share = dot(pull, hand[2], 1, 1)
+    inner = jnp.sum(share * grad_share, axis=-1, keepdims=True)
+    grad_score = (0.125 * share * (grad_share - inner)).astype(BF16)
+    ghand[:, :NARROW] = one_head(dot(grad_score, hand[1])).astype(BF16)
+    ghand[:, NARROW : 2 * NARROW] = dot(grad_score, two_heads(hand[0]), 0, 0).astype(BF16)
+    ghand[:, 2 * NARROW :] = dot(share.astype(BF16), pull, 0, 0).astype(BF16)
 
     mine = (3 - c, c)
     other = (2 + c, 1 - c)
@@ -338,15 +386,16 @@
 
     for n in range(NT):
         rows = slice(n * NARROW, (n + 1) * NARROW)
-        part[2, rows, :] = dot(tft[n], gcat[:, 2 * NARROW :]).astype(BF16)
+        part[2, rows, :] = (wacc[2, rows, :] + dot(thand[n], ghand[:, 2 * NARROW :])).astype(BF16)
         part[3, rows, :] = (gowacc[n] + dot(attx[ROWS:, :], gf[n, ROWS:, :], 0, 0)).astype(BF16)
     go(core_msg(0))
     for n in range(NT):
         rows = slice(n * NARROW, (n + 1) * NARROW)
-        grads = dot(tft[n], gcat[:, : 2 * NARROW])
-        part[0, rows, :] = grads[:, :NARROW].astype(BF16)
-        part[1, rows, :] = grads[:, NARROW:].astype(BF16)
+        grads = dot(thand[n], ghand[:, : 2 * NARROW])
+        part[0, rows, :] = (wacc[0, rows, :] + grads[:, :NARROW]).astype(BF16)
+        part[1, rows, :] = (wacc[1, rows, :] + grads[:, NARROW:]).astype(BF16)
     go(core_msg(1))
+    za[1]()
 
     def reduce_y(buf, land, which):
         def plan(kind, way):
@@ -499,6 +548,7 @@
     core_sum(1)
     x_send(1)
 
+    gcat[...] = (gcat[...].astype(F32) + dot(move[:, ROWS:], ghand[...])).astype(BF16)
     for n in range(NT):
         weight = jnp.concatenate([wi[j, n * NARROW : (n + 1) * NARROW, :] for j in range(3)], axis=1)
         pback[n] = dot(gcat[...], weight, 1, 1).astype(BF16)
@@ -613,13 +663,20 @@
             buf(ROWS, EXTRA),
             buf(3, ROWS, NARROW),
             buf(ROWS, NARROW),
-            buf(EXTRA, NARROW),
+            buf(ROWS, NARROW),
             buf(3, 2 * CAP, 2 * CAP, dtype=F32),
             buf(ROWS, NARROW),
             buf(EXTRA, NARROW),
             buf(ROWS, 3 * NARROW),
             buf(2, ROWS, NARROW, dtype=F32),
+            buf(ROWS, 3 * NARROW, dtype=F32),
+            buf(ROWS, NARROW, dtype=F32),
             buf(NT, NARROW, NARROW, dtype=F32),
+            buf(3, 1024, NARROW, dtype=F32),
+            buf(3, CAP, NARROW),
+            buf(NT, NARROW, CAP),
+            buf(2 * CAP, CAP, dtype=F32),
+            buf(CAP, 3 * NARROW),
             buf(ROWS, NARROW),
             buf(ROWS, NARROW),
             buf(4, 1024, NARROW),

time: 89.8 us -> 89.1 us (level)
  no operation moved by 1% of the time
where the time goes in v4:
time: 89.1 us; the launch traced here: 88.8 us
  Pallas kernels  88.2 us (99%)
    pallas_call x1, Pallas kernels, on_device(): pl.pallas_call(kernel, out_shape=(rows_bf16, rows_bf16, jax.ShapeDtypeStr...  85.7 us
    pallas_call x1, Pallas kernels, on_device(): pl.pallas_call(finish, out_shape=(rows_bf16, rows_bf16, jax.ShapeDtypeStr...  2.45 us

profile of v4, /device:TPU:1, one launch (start us, length us, event | category | flops | bytes accessed | tf_op | source)
XLA Modules:
  0.0 88.8 jit_solution(6737446886101389762)
XLA Ops:
  0.6 85.7 %shard_map.93 = (bf16[384,128]{1,0:T(8,128)(2,1)}, bf16[384,128]{1,0:T(8,128)(2,1)}, bf16[4,1024,128]{2,1,0:T(8,128)(2,1)}) custom-call(bf16[384,128]{1,0:T(8,128)(2,1)} %tok.1, bf16[3,1024,128]{2,1,0:T(8,128)(2,1)} %bitcast.4, bf16[128,1024]{1,0:T(8,128)(2,1)} %wo_hbm.1, bf16[384,128]{1,0:T(8,128)(2,1)} %gl.1, s32[3,128]{1,0:T(4,128)} %bitcast.5, ...), custom_call_target="tpu_custom_call" | custom-call | tf_op jit(solution)/shard_map/pallas_call | solution.py:648
  86.4 2.5 %shard_map.94 = (bf16[384,128]{1,0:T(8,128)(2,1)}, bf16[384,128]{1,0:T(8,128)(2,1)}, f32[3,1024,128]{2,1,0:T(8,128)}, f32[128,1024]{1,0:T(8,128)}) custom-call(bf16[384,128]{1,0:T(8,128)(2,1)} %get-tuple-element.11.lay_i, bf16[384,128]{1,0:T(8,128)(2,1)} %get-tuple-element.12.gtok_i, bf16[4,1024,128]{2,1,0:T(8,128)(2,1)} %get-tuple-element.13.sum_i), custom_call_target="tpu_custom_call" | custom-call | tf_op jit(solution)/shard_map/pallas_call | solution.py:718
